TPU v7x, 512 devices: a whole 4x4x16 slice. The times are simulated.
512 devices in a mesh: group: 16 (over z_lo, y), vocab: 32 (over x, z_hi, core).
Axes of the slice: x: 4, y: 4, z: 16 (z_hi: 4, z_lo: 4; z = z_hi * 4 + z_lo), core: 2. Of those that a mesh axis runs over, the one named last changes fastest.
Arguments:
- teacher_rows: bfloat16 [4096, 4096], P(('group', 'vocab')), may hold values from -8 to 8
- student_rows: bfloat16 [4096, 5120], P(('group', 'vocab')), may hold values from -8 to 8
- teacher_gain: bfloat16 [4096], replicated, may hold values from 0.25 to 1.75
- student_gain: bfloat16 [5120], replicated, may hold values from 0.25 to 1.75
- teacher_head: bfloat16 [4096, 8192], P(None, 'vocab'), may hold values from -8 to 8
- student_head: bfloat16 [5120, 8192], P(None, 'vocab'), may hold values from -8 to 8
- route: int32 [4096], replicated, may hold values from 0 to 15, as said below
- target: int32 [4096], P('group'), may hold values from 0 to 8191
Outputs:
- token_loss: float32 [4096], P('group')
- row_grad: bfloat16 [4096, 5120], P(('group', 'vocab'))
Inputs may be any that keep to these rules, and one draw needn't show every extreme that they name: route[r] is the student group of teacher row r. For every v, each student group receives exactly 8 of the rows r with (r % 256) // 8 = v, and the 8 rows t * 256 + v * 8 + k of one t and v send to each student group either none or exactly 1 row.
All inputs are finite; a program needn't handle non-finite values.
Results may differ from a plain program's by a relative error of at most 0.019.
Values may be sent and summed in bfloat16 or wider, within the bound.
A program may use at most 64 MiB of HBM per device.

v0:
```python
import jax
import jax.numpy as jnp
from jax import lax
from jax.sharding import PartitionSpec as P

epsilon = 1e-06
loss_scale = 16.0
distill_mix = 0.5


def normalize_rows(rows):
    widened = rows.astype(jnp.float32)
    inverse = lax.rsqrt(jnp.mean(widened * widened, axis=1, keepdims=True) + epsilon)
    return (widened * inverse, inverse)


def contract_last(left_side, right_side):
    return lax.dot_general(
        left_side, right_side, (((1,), (1,)), ((), ())), preferred_element_type=jnp.float32
    )


def local(
    teacher_rows,
    student_rows,
    teacher_gain,
    student_gain,
    teacher_head,
    student_head,
    route,
    target,
):
    groups = lax.axis_size("group")
    vocab_count = lax.axis_size("vocab")
    local_rows = teacher_rows.shape[0]
    capacity = max(1, local_rows // groups)
    shard_width = teacher_head.shape[1]
    my_group = lax.axis_index("group")
    my_vocab = lax.axis_index("vocab")
    route_table = route.reshape(groups, vocab_count, local_rows)
    teacher_normed = (normalize_rows(teacher_rows)[0] * teacher_gain.astype(jnp.float32)).astype(
        jnp.bfloat16
    )
    my_routes = lax.dynamic_index_in_dim(
        lax.dynamic_index_in_dim(route_table, my_group, 0, keepdims=False),
        my_vocab,
        0,
        keepdims=False,
    )
    positions = jnp.arange(local_rows)
    same_route = my_routes[:, None] == my_routes[None, :]
    earlier = positions[:, None] < positions[None, :]
    rank_within = jnp.sum(jnp.where(same_route & earlier, 1, 0), axis=0)
    slot_number = my_routes * capacity + rank_within
    send_pick = (jnp.arange(groups * capacity)[:, None] == slot_number[None, :]).astype(
        jnp.bfloat16
    )
    outgoing = jnp.dot(send_pick, teacher_normed, preferred_element_type=jnp.float32).astype(
        jnp.bfloat16
    )
    outgoing = outgoing.reshape(groups, capacity, teacher_normed.shape[1])
    incoming = lax.all_to_all(outgoing, "group", split_axis=0, concat_axis=0, tiled=True)
    column = lax.dynamic_index_in_dim(route_table, my_vocab, 1, keepdims=False)
    counts = jnp.sum(jnp.where(column == my_group, 1, 0), axis=1)
    group_number = jnp.arange(groups)
    before = jnp.sum(
        jnp.where(group_number[:, None] > group_number[None, :], counts[None, :], 0), axis=1
    )
    slot_index = jnp.arange(capacity)
    is_valid = slot_index[None, :] < counts[:, None]
    target_place = jnp.where(is_valid, before[:, None] + slot_index[None, :], -1).reshape(
        groups * capacity
    )
    receive_pick = (positions[:, None] == target_place[None, :]).astype(jnp.bfloat16)
    routed = jnp.dot(
        receive_pick, incoming.reshape(groups * capacity, -1), preferred_element_type=jnp.float32
    ).astype(jnp.bfloat16)
    student_hat, inverse = normalize_rows(student_rows)
    gain_wide = student_gain.astype(jnp.float32)
    student_normed = (student_hat * gain_wide).astype(jnp.bfloat16)
    teacher_logits = jnp.dot(
        lax.all_gather(routed, "vocab", axis=0, tiled=True),
        teacher_head,
        preferred_element_type=jnp.float32,
    )
    student_logits = jnp.dot(
        lax.all_gather(student_normed, "vocab", axis=0, tiled=True),
        student_head,
        preferred_element_type=jnp.float32,
    )
    columns = my_vocab * shard_width + jnp.arange(shard_width)
    is_target = columns[None, :] == target[:, None]
    teacher_top, student_top = lax.pmax(
        (jnp.max(teacher_logits, axis=1), jnp.max(student_logits, axis=1)), "vocab"
    )
    teacher_exp = jnp.exp(teacher_logits - teacher_top[:, None])
    student_exp = jnp.exp(student_logits - student_top[:, None])
    teacher_sum, student_sum, cross_sum, picked = lax.psum(
        (
            jnp.sum(teacher_exp, axis=1),
            jnp.sum(student_exp, axis=1),
            jnp.sum(teacher_exp * (teacher_logits - student_logits), axis=1),
            jnp.sum(jnp.where(is_target, student_logits, 0.0), axis=1),
        ),
        "vocab",
    )
    teacher_lse = teacher_top + jnp.log(teacher_sum)
    student_lse = student_top + jnp.log(student_sum)
    token_loss = distill_mix * (cross_sum / teacher_sum - teacher_lse + student_lse) + (
        1.0 - distill_mix
    ) * (student_lse - picked)
    logit_grad = (
        loss_scale
        * (
            student_exp / student_sum[:, None]
            - distill_mix * teacher_exp / teacher_sum[:, None]
            - (1.0 - distill_mix) * jnp.where(is_target, 1.0, 0.0)
        )
    ).astype(jnp.bfloat16)
    head_grad = lax.psum_scatter(
        contract_last(logit_grad, student_head).astype(jnp.bfloat16),
        "vocab",
        scatter_dimension=0,
        tiled=True,
    ).astype(jnp.float32)
    scaled_grad = head_grad * gain_wide
    row_grad = inverse * (
        scaled_grad - student_hat * jnp.mean(scaled_grad * student_hat, axis=1, keepdims=True)
    )
    return (token_loss, row_grad.astype(jnp.bfloat16))


def solution(mesh):
    placed = (
        P(("group", "vocab"), None),
        P(("group", "vocab"), None),
        P(),
        P(),
        P(None, "vocab"),
        P(None, "vocab"),
        P(),
        P("group"),
    )
    return jax.shard_map(
        local,
        mesh=mesh,
        in_specs=placed,
        out_specs=(P("group"), P(("group", "vocab"), None)),
        check_vma=False,
    )
```

profile of v0, /device:TPU:24, one launch (start us, length us, event | category | flops | bytes accessed | tf_op | source)
XLA Modules:
  0.0 495.1 jit_solution(16316269187809809975)
XLA Ops:
  7.2 0.0 copy-start
  7.2 1.1 fusion.18
  8.3 0.7 convert_element_type.39
  9.0 0.9 reshape.72
  9.9 0.1 select_reduce_fusion.1
  10.0 1.1 fusion
  11.1 0.5 broadcast.93
  11.6 0.7 reduce.1
  12.3 0.7 reshape.75
  13.0 8.9 %all-to-all-start = ((bf16[16,2,2048]{2,1,0:T(2,128)(2,1)}), bf16[16,2,2048]{2,1,0:T(2,128)(2,1)S(1)}, u32[]{:S(2)}, u32[]{:S(2)}) async-start(bf16[16,2,2048]{2,1,0:T(2,128)(2,1)} %reshape.75), calls=%async_computation | async-start | bytes 262144 | tf_op jit(solution)/shard_map/all_to_all | solution.py:62
  21.9 0.0 all-gather.3.cloned.1.call-start
  22.0 0.4 fusion.36
  22.4 0.1 select_reduce_fusion
  22.5 5.6 %all-to-all-done = bf16[16,2,2048]{2,1,0:T(2,128)(2,1)S(1)} async-done(((bf16[16,2,2048]{2,1,0:T(2,128)(2,1)}), bf16[16,2,2048]{2,1,0:T(2,128)(2,1)S(1)}, u32[]{:S(2)}, u32[]{:S(2)}) %all-to-all-start) | async-done | bytes 131104 | tf_op jit(solution)/shard_map/all_to_all | solution.py:62
  28.1 0.1 reshape.76
  28.2 0.9 convolution_convert_fusion.2
  29.1 0.0 all-gather.3.cloned.1.call-update
  29.1 0.0 all-gather.5.cloned.1.call-start
  29.1 0.7 convert_element_type.44
  29.9 1.0 fusion.16
  30.9 1.6 fusion.11
  32.5 0.0 all-gather.5.cloned.1.call-update
  32.5 0.0 reduce-scatter.2.cloned.1.call-start
  32.6 76.8 %all-gather.3.cloned.1.call-done = bf16[256,4096]{1,0:T(8,128)(2,1)} async-done(((bf16[8,4096]{1,0:T(8,128)(2,1)}), bf16[256,4096]{1,0:T(8,128)(2,1)}) %all-gather.3.cloned.1.call-update) | async-done | bytes 2097168 | tf_op jit(solution)/shard_map/all_gather | solution.py:82
  109.4 3.2 fusion.44
  112.6 0.0 copy-start.2
  112.6 78.4 %all-gather.5.cloned.1.call-done = bf16[256,5120]{1,0:T(8,128)(2,1)} async-done(((bf16[8,5120]{1,0:T(8,128)(2,1)}), bf16[256,5120]{1,0:T(8,128)(2,1)}) %all-gather.5.cloned.1.call-update) | async-done | bytes 2621456 | tf_op jit(solution)/shard_map/all_gather | solution.py:87
  191.0 0.0 copy-done
  191.0 2.9 fusion.45
  193.9 87.1 %all-reduce.1 = (f32[256]{0:T(256)S(1)}, f32[256]{0:T(256)S(1)}) all-reduce(f32[256]{0:T(256)S(1)} %get-tuple-element.12, f32[256]{0:T(256)S(1)} %get-tuple-element.14), channel_id=1, replica_groups=mesh['group'=16,'vocab'=32] {'vocab'}, use_global_device_ids=true, to_apply=%region_5.6 | all-reduce | flops 512 | bytes 4096 | tf_op jit(solution)/shard_map/pmax | solution.py:93
  281.0 0.0 copy-done.2
  281.0 0.1 multiply_reduce_fusion
  281.1 84.2 %all-reduce = (f32[256]{0:T(256)S(1)}, f32[256]{0:T(256)S(1)}, f32[256]{0:T(256)S(1)}, f32[256]{0:T(256)S(1)}) all-reduce(f32[256]{0:T(256)S(1)} %get-tuple-element.4, f32[256]{0:T(256)S(1)} %get-tuple-element.5, f32[256]{0:T(256)S(1)} %get-tuple-element.3, ...), channel_id=1, replica_groups=mesh['group'=16,'vocab'=32] {'vocab'}, use_global_device_ids=true, to_apply=%region_16.17 | all-reduce | flops 1024 | bytes 8192 | tf_op jit(solution)/shard_map/psum | solution.py:98
  365.4 2.5 convolution_convert_fusion
  367.9 0.0 copy-start.1
  367.9 0.0 reduce-scatter.2.cloned.1.call-update
  367.9 0.6 add_multiply_fusion
  368.5 117.3 %reduce-scatter.2.cloned.1.call-done = bf16[8,5120]{1,0:T(8,128)(2,1)} async-done(((bf16[256,5120]{1,0:T(8,128)(2,1)}), bf16[8,5120]{1,0:T(8,128)(2,1)}) %reduce-scatter.2.cloned.1.call-update) | async-done | bytes 81936 | tf_op jit(solution)/shard_map/reduce_scatter | solution.py:120
  485.8 0.0 copy-done.1
  485.8 1.1 fusion.12
  486.9 1.6 fusion.15
  (7 shorter events, 0.1 us)
Async XLA Ops:
  7.2 183.8 %copy-start = (bf16[5120,256]{1,0:T(8,128)(2,1)S(1)}, bf16[5120,256]{1,0:T(8,128)(2,1)}, u32[]{:S(2)}) copy-start(bf16[5120,256]{1,0:T(8,128)(2,1)} %param.13) | copy-start | bytes 7864324
  13.0 15.1 %all-to-all-start = ((bf16[16,2,2048]{2,1,0:T(2,128)(2,1)}), bf16[16,2,2048]{2,1,0:T(2,128)(2,1)S(1)}, u32[]{:S(2)}, u32[]{:S(2)}) async-start(bf16[16,2,2048]{2,1,0:T(2,128)(2,1)} %reshape.75), calls=%async_computation | async-start | bytes 262144 | tf_op jit(solution)/shard_map/all_to_all | solution.py:62
  21.9 87.5 %all-gather.3.cloned.1.call-start = ((), (), s32[]{:S(2)}) async-start(), calls=%async_computation.2 | async-start | bytes 2162688 | tf_op jit(solution)/shard_map/all_gather | solution.py:82
  29.1 161.9 %all-gather.5.cloned.1.call-start = ((), (), s32[]{:S(2)}) async-start(), calls=%async_computation.3 | async-start | bytes 2703360 | tf_op jit(solution)/shard_map/all_gather | solution.py:87
  32.5 453.3 %reduce-scatter.2.cloned.1.call-start = ((), (), s32[]{:S(2)}) async-start(), calls=%async_computation.4 | async-start | bytes 2703360 | tf_op jit(solution)/shard_map/reduce_scatter | solution.py:120
  112.6 168.4 %copy-start.2 = (s32[256]{0:T(256)S(1)}, s32[256]{0:T(256)}, u32[]{:S(2)}) copy-start(s32[256]{0:T(256)} %param.15) | copy-start | bytes 3076
  367.9 117.9 %copy-start.1 = (bf16[8,5120]{1,0:T(8,128)(2,1)S(1)}, bf16[8,5120]{1,0:T(8,128)(2,1)}, u32[]{:S(2)}) copy-start(bf16[8,5120]{1,0:T(8,128)(2,1)} %param.9) | copy-start | bytes 245764
Sparse Core Ops, SparseCore 0:
  29.2 80.1 all-gather.2
  113.1 77.8 all-gather.4
  368.1 117.6 reduce-scatter.1
where the time goes:
time: 496 us; the launch traced here: 495 us
  waiting for transfers between devices  278 us (56%)
  blocking collectives  171 us (34%)
  between operations  13.8 us (3%)
  matrix products  10.5 us (2%)
  other arithmetic  9.97 us (2%)
  starting transfers between devices  9.03 us (2%)
    reduce_scatter x1, waiting for transfers between devices, local(): lax.psum_scatter(contract_last(logit_grad, student_head).astype(jnp.bfloa...  117 us
    pmax x1, blocking collectives, local(): lax.pmax((jnp.max(teacher_logits, axis=1), jnp.max(student_logits, axis=1...  87.1 us
    psum x1, blocking collectives, local(): lax.psum((jnp.sum(teacher_exp, axis=1), jnp.sum(student_exp, axis=1), jnp...  84.2 us
    all_gather x1, waiting for transfers between devices, local(): lax.all_gather(student_normed, 'vocab', axis=0, tiled=True)  78.4 us
    all_gather x1, waiting for transfers between devices, local(): lax.all_gather(routed, 'vocab', axis=0, tiled=True)  76.8 us
  transfers between devices with their start and end apart: 4, of which 4 were waited for; matrix products, arithmetic and copies ran while one was open for 2% of the time, Pallas kernels for 0%

commit v1 on v0

v1 whole, which is shorter than its diff:
```python
import functools

import jax
import jax.numpy as jnp
from jax import lax
from jax.experimental import pallas as pl
from jax.experimental.pallas import tpu as pltpu
from jax.sharding import PartitionSpec as P

MESH = pl.DeviceIdType.MESH
epsilon = 1e-06
loss_scale = 16.0
distill_mix = 0.5

RING = 4
CORES = 2
SUB = 16


def contract_last(left_side, right_side):
    return lax.dot_general(
        left_side, right_side, (((1,), (1,)), ((), ())), preferred_element_type=jnp.float32
    )


class Gather:
    def __init__(self, buf, send, recv, place):
        self.buf, self.send, self.recv, self.place = buf, send, recv, place
        self.started = []
        self.core_left = []

    def copy(self, index, cols, xx, zz, dev):
        view = self.buf.at[cols, self.place.rows(xx, zz), :]
        return pltpu.make_async_remote_copy(
            src_ref=view,
            dst_ref=view,
            send_sem=self.send.at[index],
            recv_sem=self.recv.at[index],
            device_id=dev,
            device_id_type=MESH,
        )

    def go(self, *args):
        copy = self.copy(*args)
        copy.start()
        self.started.append(copy)
        return copy

    def half(self):
        return pl.ds(self.place.core * 2, 2)

    def quarter(self, h):
        return pl.ds(self.place.core * 2 + h, 1)

    def z_near(self):
        p = self.place
        self.zp = self.go(0, self.half(), p.x, p.zh, p.dev(p.x, p.zh + 1, p.core))
        self.zm = self.go(1, self.half(), p.x, p.zh, p.dev(p.x, p.zh - 1, p.core))
        self.x_near(0)

    def x_near(self, j):
        p = self.place
        zz = p.zh + (0, -1, 1, 2)[j]
        self.go(4 + 4 * j, self.half(), p.x, zz, p.dev(p.x + 1, p.zh, p.core))
        self.go(5 + 4 * j, self.half(), p.x, zz, p.dev(p.x - 1, p.zh, p.core))

    def to_core(self, index, xx, zz):
        p = self.place
        self.core_left.append(self.go(index, self.half(), xx, zz, p.dev(p.x, p.zh, 1 - p.core)))

    def z_from_minus(self):
        p = self.place
        self.zp.wait_recv()
        self.zfp = self.go(2, self.quarter(0), p.x, p.zh - 1, p.dev(p.x, p.zh + 1, p.core))
        self.x_near(1)
        self.to_core(20, p.x, p.zh - 1)

    def z_from_plus(self):
        p = self.place
        self.zm.wait_recv()
        self.zfm = self.go(3, self.quarter(1), p.x, p.zh + 1, p.dev(p.x, p.zh - 1, p.core))
        self.x_near(2)
        self.to_core(21, p.x, p.zh + 1)

    def z_far(self):
        p = self.place
        self.zfp.wait_recv()
        self.zfm.wait_recv()
        self.x_near(3)
        self.to_core(22, p.x, p.zh + 2)

    def x_from_near(self, j):
        p = self.place
        zz = p.zh + (0, -1, 1, 2)[j]
        plus, minus = p.dev(p.x + 1, p.zh, p.core), p.dev(p.x - 1, p.zh, p.core)
        self.copy(4 + 4 * j, self.half(), p.x - 1, zz, plus).wait_recv()
        self.go(6 + 4 * j, self.quarter(0), p.x - 1, zz, plus)
        self.to_core(23 + 3 * j, p.x - 1, zz)
        self.copy(5 + 4 * j, self.half(), p.x + 1, zz, minus).wait_recv()
        self.go(7 + 4 * j, self.quarter(1), p.x + 1, zz, minus)
        self.to_core(24 + 3 * j, p.x + 1, zz)

    def x_far(self, j):
        p = self.place
        zz = p.zh + (0, -1, 1, 2)[j]
        plus, minus = p.dev(p.x + 1, p.zh, p.core), p.dev(p.x - 1, p.zh, p.core)
        self.copy(6 + 4 * j, self.quarter(0), p.x + 2, zz, plus).wait_recv()
        self.copy(7 + 4 * j, self.quarter(1), p.x + 2, zz, minus).wait_recv()
        self.to_core(25 + 3 * j, p.x + 2, zz)

    def from_core(self):
        for copy in self.core_left:
            copy.wait_recv()


GATHER_COPIES = 35


class Place:
    def __init__(self):
        self.group = lax.axis_index("group")
        self.vocab = lax.axis_index("vocab")
        self.core = lax.rem(self.vocab, CORES)
        self.zh = lax.rem(self.vocab // CORES, RING)
        self.x = self.vocab // (CORES * RING)

    def dev(self, xx, zz, cc):
        xx, zz = lax.rem(xx + RING, RING), lax.rem(zz + RING, RING)
        return (self.group, (xx * RING + zz) * CORES + cc)

    def rows(self, xx, zz):
        xx, zz = lax.rem(xx + RING, RING), lax.rem(zz + RING, RING)
        return pl.ds(pl.multiple_of((xx * RING + zz) * 16, 16), 16)


def kernel(
    groups,
    teacher_rows,
    student_rows,
    teacher_gain,
    student_gain,
    teacher_head,
    student_head,
    route,
    target,
    loss_out,
    grad_out,
    head_t,
    head_s,
    rows_t,
    rows_s,
    wide,
    out_rows,
    in_rows,
    pair_t_out,
    pair_t_in,
    pair_s_out,
    pair_s_in,
    inverse_keep,
    exp_t,
    exp_s,
    keep_s,
    logit_grad,
    stat_one,
    stat_two,
    own_part,
    pair_out,
    pair_in,
    xf_out,
    xf_in,
    xn_out,
    xn_in,
    z_part,
    zf_out,
    zf_in,
    zn_out,
    zn_in,
    mine,
    last_out,
    last_in,
    local_sem,
    pair_sem,
    route_sem,
    gather_t_sem,
    gather_s_sem,
    stat_sem,
    back_sem,
):
    p = Place()
    g, v, core, zh, x = p.group, p.vocab, p.core, p.zh, p.x
    local_rows = teacher_rows.shape[0]
    dt, ds = teacher_rows.shape[1], student_rows.shape[1]
    wt, ws = dt // 4, ds // 4
    chunk = dt // SUB
    other = p.dev(x, zh, 1 - core)
    f32, bf16 = jnp.float32, jnp.bfloat16
    sends = []

    def remote(src, dst, sem, index, dev):
        copy = pltpu.make_async_remote_copy(
            src_ref=src,
            dst_ref=dst,
            send_sem=sem.at[0, index],
            recv_sem=sem.at[1, index],
            device_id=dev,
            device_id_type=MESH,
        )
        copy.start()
        sends.append(copy)
        return copy

    barrier = pltpu.get_barrier_semaphore()
    flat = x * CORES + core

    def near(d):
        f = lax.rem(flat + d, RING * CORES)
        return f

    def near_dev(d):
        f = near(d)
        return p.dev(f // CORES, zh, lax.rem(f, CORES))

    for d in range(1, groups):
        pl.semaphore_signal(
            barrier, inc=1, device_id=(lax.rem(g + d, groups), v), device_id_type=MESH
        )
    for d in range(1, RING):
        pl.semaphore_signal(
            barrier, inc=1, device_id=p.dev(x, zh + d, core), device_id_type=MESH
        )
    for d in range(1, RING * CORES):
        pl.semaphore_signal(barrier, inc=1, device_id=near_dev(d), device_id_type=MESH)

    load_s = pltpu.make_async_copy(student_head, head_s, local_sem.at[0])
    load_t = pltpu.make_async_copy(teacher_head, head_t, local_sem.at[1])
    load_s.start()
    load_t.start()

    wide_s = student_rows[...].astype(f32)
    inverse = lax.rsqrt(jnp.mean(wide_s * wide_s, axis=1, keepdims=True) + epsilon)
    inverse_keep[...] = jnp.broadcast_to(inverse, inverse_keep.shape)
    pair_s_out[...] = (
        (wide_s * inverse * student_gain[...].astype(f32)).astype(bf16).astype(f32)
    )
    wide_t = teacher_rows[...].astype(f32)
    inverse_t = lax.rsqrt(jnp.mean(wide_t * wide_t, axis=1, keepdims=True) + epsilon)
    normed_t = (wide_t * inverse_t * teacher_gain[...].astype(f32)).astype(bf16).astype(f32)
    for c in range(SUB):
        wide[:, c, :] = normed_t[:, c * chunk : (c + 1) * chunk]
    first = (g * lax.axis_size("vocab") + v) * local_rows
    my_routes = [route[first + k] for k in range(local_rows)]

    @pl.loop(0, groups)
    def _(dest):
        total = jnp.zeros((SUB, chunk), f32)
        for k in range(local_rows):
            total += jnp.where(my_routes[k] == dest, 1.0, 0.0) * wide[k]
        out_rows[dest] = total.astype(bf16)

    in_rows[g] = out_rows[g]

    pl.semaphore_wait(barrier, groups - 1 + RING - 1 + RING * CORES - 1)

    pair_s = remote(pair_s_out, pair_s_in, pair_sem, 0, other)
    routed_copies = []
    for d in range(1, groups):
        dest = lax.rem(g + d, groups)
        routed_copies.append(
            remote(out_rows.at[dest], in_rows.at[g], route_sem, d, (dest, v))
        )

    def own_block(rows, pair_out_ref, pair_in_ref, width):
        mine_rows, their_rows = pair_out_ref[...], pair_in_ref[...]
        is_first = core == 0
        both = jnp.concatenate(
            [
                jnp.where(is_first, mine_rows, their_rows),
                jnp.where(is_first, their_rows, mine_rows),
            ],
            axis=0,
        ).astype(bf16)
        for q in range(4):
            rows[q, p.rows(x, zh), :] = both[:, q * width : (q + 1) * width]

    student = Gather(rows_s, gather_s_sem.at[0], gather_s_sem.at[1], p)
    teacher = Gather(rows_t, gather_t_sem.at[0], gather_t_sem.at[1], p)

    pair_s.wait_recv()
    own_block(rows_s, pair_s_out, pair_s_in, ws)
    student.z_near()

    ranks, valids = [], []
    seen = jnp.int32(0)
    for t in range(groups):
        start = (t * lax.axis_size("vocab") + v) * local_rows
        valid = jnp.int32(0)
        for k in range(local_rows):
            valid += jnp.where(route[start + k] == g, 1, 0)
        ranks.append(seen)
        valids.append(valid)
        seen = seen + valid
    for copy in routed_copies:
        copy.wait_recv()
    for j in range(local_rows):
        total = jnp.zeros((SUB, chunk), f32)
        for t in range(groups):
            weight = jnp.where(ranks[t] == j, valids[t], 0).astype(f32)
            total += weight * in_rows[t].astype(f32)
        wide[j] = total
    for c in range(SUB):
        pair_t_out[:, c * chunk : (c + 1) * chunk] = wide[:, c, :]
    pair_t = remote(pair_t_out, pair_t_in, pair_sem, 1, other)
    pair_t.wait_recv()
    own_block(rows_t, pair_t_out, pair_t_in, wt)
    teacher.z_near()

    student.z_from_minus()
    student.z_from_plus()
    student.x_from_near(0)
    student.x_far(0)
    student.z_far()
    student.x_from_near(1)
    student.x_from_near(2)
    teacher.z_from_minus()
    teacher.z_from_plus()
    student.x_far(1)
    student.x_far(2)
    student.x_from_near(3)
    teacher.x_from_near(0)
    teacher.x_far(0)
    student.x_far(3)
    student.from_core()
    teacher.z_far()
    teacher.x_from_near(1)
    teacher.x_from_near(2)

    load_s.wait()
    total = jnp.zeros((logit_grad.shape[0], head_s.shape[1]), f32)
    for q in range(4):
        total += jnp.dot(
            rows_s[q], head_s[q * ws : (q + 1) * ws, :], preferred_element_type=f32
        )
    logits_s = jnp.transpose(total)
    top_s = jnp.max(logits_s, axis=0, keepdims=True)
    keep_s[...] = logits_s
    powers = jnp.exp(logits_s - top_s)
    exp_s[...] = powers
    sum_s = jnp.sum(powers, axis=0, keepdims=True)
    shard = head_s.shape[1]
    columns = v * shard + lax.broadcasted_iota(jnp.int32, exp_s.shape, 0)
    picked = jnp.sum(
        jnp.where(columns == target[...], logits_s, 0.0), axis=0, keepdims=True
    )

    teacher.x_far(1)
    teacher.x_far(2)
    teacher.x_from_near(3)
    teacher.x_far(3)
    teacher.from_core()

    load_t.wait()
    total = jnp.zeros((logit_grad.shape[0], head_t.shape[1]), f32)
    for q in range(4):
        total += jnp.dot(
            rows_t[q], head_t[q * wt : (q + 1) * wt, :], preferred_element_type=f32
        )
    logits_t = jnp.transpose(total)
    top_t = jnp.max(logits_t, axis=0, keepdims=True)
    powers = jnp.exp(logits_t - top_t)
    exp_t[...] = powers
    sum_t = jnp.sum(powers, axis=0, keepdims=True)
    cross = jnp.sum(powers * (logits_t - keep_s[...]), axis=0, keepdims=True)

    stats = jnp.concatenate(
        [top_t, top_s, top_t, jnp.zeros_like(top_t), sum_t, sum_s, cross, picked], axis=0
    )

    def merge(slots, count):
        parts = [slots[i] for i in range(count)]
        top = functools.reduce(jnp.maximum, [part[0:4] for part in parts])
        sums = sum(jnp.exp(part[0:4] - top) * part[4:8] for part in parts)
        return jnp.concatenate([top, sums], axis=0)

    stat_one[flat] = stats
    copies = [
        remote(stat_one.at[flat], stat_one.at[flat], stat_sem, d, near_dev(d))
        for d in range(1, RING * CORES)
    ]
    for copy in copies:
        copy.wait_recv()
    stat_two[zh] = merge(stat_one, RING * CORES)
    copies = [
        remote(
            stat_two.at[zh],
            stat_two.at[zh],
            stat_sem,
            RING * CORES + d,
            p.dev(x, zh + d, core),
        )
        for d in range(1, RING)
    ]
    for copy in copies:
        copy.wait_recv()
    merged = merge(stat_two, RING)
    all_top_t, all_top_s = merged[0:1], merged[1:2]
    all_sum_t, all_sum_s = merged[4:5], merged[5:6]
    scale_s = loss_scale * jnp.exp(top_s - all_top_s) / all_sum_s
    scale_t = (loss_scale * distill_mix) * jnp.exp(top_t - all_top_t) / all_sum_t
    gradient = (
        exp_s[...] * scale_s
        - exp_t[...] * scale_t
        - jnp.where(columns == target[...], loss_scale * (1.0 - distill_mix), 0.0)
    )
    logit_grad[...] = jnp.transpose(gradient).astype(bf16)

    order = (2, 1, -1, 0)
    plus_x, minus_x = p.dev(x + 1, zh, core), p.dev(x - 1, zh, core)
    plus_z, minus_z = p.dev(x, zh + 1, core), p.dev(x, zh - 1, core)
    pair_copies, far_copies, near_copies = {}, {}, {}

    def head_quarter(q):
        return head_s[pl.ds(pl.multiple_of(q * ws, ws), ws), :]

    def multiply(i):
        zz = zh + order[i]
        left = jnp.concatenate(
            [logit_grad[p.rows(x + d, zz), :] for d in order], axis=0
        )
        for h in range(2):
            pair_out[i, h] = contract_last(
                left, head_quarter((1 - core) * 2 + h)
            ).astype(bf16)
        pair_copies[i] = remote(pair_out.at[i], pair_in.at[i], back_sem, i, other)
        for h in range(2):
            own_part[i, h] = contract_last(left, head_quarter(core * 2 + h))

    def x_far(i):
        pair_copies[i].wait_recv()
        own_part[i] = own_part[i] + pair_in[i].astype(f32)
        xf_out[i] = own_part[i, :, 0:16, :].astype(bf16)
        far_copies[i] = (
            remote(xf_out.at[i, 0], xf_in.at[i, 0], back_sem, 4 + 2 * i, plus_x),
            remote(xf_out.at[i, 1], xf_in.at[i, 1], back_sem, 5 + 2 * i, minus_x),
        )

    def x_near(i):
        far_copies[i][0].wait_recv()
        xn_out[i, 0, 0] = (own_part[i, 0, 16:32, :] + xf_in[i, 0].astype(f32)).astype(bf16)
        xn_out[i, 0, 1] = own_part[i, 1, 16:32, :].astype(bf16)
        up = remote(xn_out.at[i, 0], xn_in.at[i, 0], back_sem, 12 + 2 * i, plus_x)
        far_copies[i][1].wait_recv()
        xn_out[i, 1, 0] = own_part[i, 0, 32:48, :].astype(bf16)
        xn_out[i, 1, 1] = (own_part[i, 1, 32:48, :] + xf_in[i, 1].astype(f32)).astype(bf16)
        down = remote(xn_out.at[i, 1], xn_in.at[i, 1], back_sem, 13 + 2 * i, minus_x)
        near_copies[i] = (up, down)

    def x_done(i):
        for copy in near_copies[i]:
            copy.wait_recv()
        return (
            own_part[i, :, 48:64, :] + xn_in[i, 0].astype(f32) + xn_in[i, 1].astype(f32)
        )

    multiply(0)
    multiply(1)
    x_far(0)
    multiply(2)
    x_far(1)
    x_near(0)
    multiply(3)
    x_far(2)
    x_near(1)
    zf_out[...] = x_done(0).astype(bf16)
    z_far = (
        remote(zf_out.at[0], zf_in.at[0], back_sem, 20, plus_z),
        remote(zf_out.at[1], zf_in.at[1], back_sem, 21, minus_z),
    )
    x_far(3)
    x_near(2)
    z_part[0] = x_done(1)
    z_far[0].wait_recv()
    zn_out[0, 0] = (z_part[0, 0] + zf_in[0].astype(f32)).astype(bf16)
    zn_out[0, 1] = z_part[0, 1].astype(bf16)
    z_up = remote(zn_out.at[0], zn_in.at[0], back_sem, 22, plus_z)
    x_near(3)
    z_part[1] = x_done(2)
    z_far[1].wait_recv()
    zn_out[1, 0] = z_part[1, 0].astype(bf16)
    zn_out[1, 1] = (z_part[1, 1] + zf_in[1].astype(f32)).astype(bf16)
    z_down = remote(zn_out.at[1], zn_in.at[1], back_sem, 23, minus_z)
    z_part[2] = x_done(3)

    lse_t = all_top_t + jnp.log(all_sum_t)
    lse_s = all_top_s + jnp.log(all_sum_s)
    loss_out[...] = distill_mix * (merged[6:7] / all_sum_t - lse_t + lse_s) + (
        1.0 - distill_mix
    ) * (lse_s - merged[7:8])
    inverse = inverse_keep[:, 0:1]
    hat = student_rows[...].astype(f32) * inverse
    gain = student_gain[...].astype(f32)

    z_up.wait_recv()
    z_down.wait_recv()
    mine[...] = z_part[2] + zn_in[0].astype(f32) + zn_in[1].astype(f32)
    last_out[...] = mine[:, pl.ds(pl.multiple_of((1 - core) * 8, 8), 8), :]
    last = remote(last_out, last_in, back_sem, 24, other)
    kept = mine[:, pl.ds(pl.multiple_of(core * 8, 8), 8), :]
    last.wait_recv()
    theirs = last_in[...]
    is_first = core == 0
    head_grad = jnp.concatenate(
        [
            jnp.where(is_first, kept[0], theirs[0]),
            jnp.where(is_first, kept[1], theirs[1]),
            jnp.where(is_first, theirs[0], kept[0]),
            jnp.where(is_first, theirs[1], kept[1]),
        ],
        axis=1,
    )
    scaled = head_grad * gain
    grad_out[...] = (
        inverse * (scaled - hat * jnp.mean(scaled * hat, axis=1, keepdims=True))
    ).astype(bf16)

    for copy in sends + student.started + teacher.started:
        copy.wait_send()


def local(
    teacher_rows,
    student_rows,
    teacher_gain,
    student_gain,
    teacher_head,
    student_head,
    route,
    target,
):
    groups = lax.axis_size("group")
    f32, bf16 = jnp.float32, jnp.bfloat16
    local_rows, dt = teacher_rows.shape
    ds = student_rows.shape[1]
    shard = teacher_head.shape[1]
    rows = target.shape[0]
    wt, ws, chunk = dt // 4, ds // 4, dt // SUB
    vmem = pl.BlockSpec(memory_space=pltpu.VMEM)
    hbm = pl.BlockSpec(memory_space=pl.ANY)
    loss, grad = pl.pallas_call(
        functools.partial(kernel, groups),
        out_shape=(
            jax.ShapeDtypeStruct((1, rows), f32),
            jax.ShapeDtypeStruct((local_rows, ds), bf16),
        ),
        in_specs=[
            vmem,
            vmem,
            vmem,
            vmem,
            hbm,
            hbm,
            pl.BlockSpec(memory_space=pltpu.SMEM),
            vmem,
        ],
        out_specs=(vmem, vmem),
        scratch_shapes=[
            pltpu.VMEM((dt, shard), bf16),
            pltpu.VMEM((ds, shard), bf16),
            pltpu.VMEM((4, rows, wt), bf16),
            pltpu.VMEM((4, rows, ws), bf16),
            pltpu.VMEM((local_rows, SUB, chunk), f32),
            pltpu.VMEM((groups, SUB, chunk), bf16),
            pltpu.VMEM((groups, SUB, chunk), bf16),
            pltpu.VMEM((local_rows, dt), f32),
            pltpu.VMEM((local_rows, dt), f32),
            pltpu.VMEM((local_rows, ds), f32),
            pltpu.VMEM((local_rows, ds), f32),
            pltpu.VMEM((local_rows, 128), f32),
            pltpu.VMEM((shard, rows), f32),
            pltpu.VMEM((shard, rows), f32),
            pltpu.VMEM((shard, rows), f32),
            pltpu.VMEM((rows, shard), bf16),
            pltpu.VMEM((RING * CORES, 8, rows), f32),
            pltpu.VMEM((RING, 8, rows), f32),
            pltpu.VMEM((4, 2, 64, ws), f32),
            pltpu.VMEM((4, 2, 64, ws), bf16),
            pltpu.VMEM((4, 2, 64, ws), bf16),
            pltpu.VMEM((4, 2, 16, ws), bf16),
            pltpu.VMEM((4, 2, 16, ws), bf16),
            pltpu.VMEM((4, 2, 2, 16, ws), bf16),
            pltpu.VMEM((4, 2, 2, 16, ws), bf16),
            pltpu.VMEM((3, 2, 16, ws), f32),
            pltpu.VMEM((2, 16, ws), bf16),
            pltpu.VMEM((2, 16, ws), bf16),
            pltpu.VMEM((2, 2, 16, ws), bf16),
            pltpu.VMEM((2, 2, 16, ws), bf16),
            pltpu.VMEM((2, 16, ws), f32),
            pltpu.VMEM((2, 8, ws), f32),
            pltpu.VMEM((2, 8, ws), f32),
            pltpu.SemaphoreType.DMA((2,)),
            pltpu.SemaphoreType.DMA((2, 2)),
            pltpu.SemaphoreType.DMA((2, groups)),
            pltpu.SemaphoreType.DMA((2, GATHER_COPIES)),
            pltpu.SemaphoreType.DMA((2, GATHER_COPIES)),
            pltpu.SemaphoreType.DMA((2, RING * CORES + RING)),
            pltpu.SemaphoreType.DMA((2, 25)),
        ],
        compiler_params=pltpu.CompilerParams(
            collective_id=0, has_side_effects=True, vmem_limit_bytes=48 * 1024 * 1024
        ),
        name="distill",
    )(
        teacher_rows,
        student_rows,
        teacher_gain.reshape(1, dt),
        student_gain.reshape(1, ds),
        teacher_head,
        student_head,
        route,
        target.reshape(1, rows),
    )
    return (loss.reshape(rows), grad)


def solution(mesh):
    placed = (
        P(("group", "vocab"), None),
        P(("group", "vocab"), None),
        P(),
        P(),
        P(None, "vocab"),
        P(None, "vocab"),
        P(),
        P("group"),
    )
    return jax.shard_map(
        local,
        mesh=mesh,
        in_specs=placed,
        out_specs=(P("group"), P(("group", "vocab"), None)),
        check_vma=False,
    )
```

time: 496 us -> 111 us (0.22)
  the two profiles are of different devices: /device:TPU:24 before, /device:TPU:19 now
where the time goes in v1:
time: 111 us
  Pallas kernels  101 us (91%)
  local copies, waits for them, and re-layouts  9.07 us (8%)
    pallas_call x1, Pallas kernels, local(): pl.pallas_call(functools.partial(kernel, groups), out_shape=(jax.ShapeDty...  101 us
    unnamed x14, local copies, waits for them, and re-layouts  7.65 us

profile of v1, /device:TPU:19, one launch (start us, length us, event | category | flops | bytes accessed | tf_op | source)
XLA Modules:
  0.0 110.9 jit_solution(15918073546680879605)
XLA Ops:
  0.6 0.7 reshape.16.teacher_gain
  1.3 0.7 reshape.17.student_gain
  2.1 0.0 copy-start
  2.1 1.7 %copy-done = bf16[5120,256]{1,0:T(8,128)(2,1)S(1)} copy-done((bf16[5120,256]{1,0:T(8,128)(2,1)S(1)}, bf16[5120,256]{1,0:T(8,128)(2,1)}, u32[]{:S(2)}) %copy-start) | copy-done | bytes 2621464
  3.8 0.0 copy-start.1
  3.8 1.6 %copy-done.1 = bf16[4096,256]{1,0:T(8,128)(2,1)S(1)} copy-done((bf16[4096,256]{1,0:T(8,128)(2,1)S(1)}, bf16[4096,256]{1,0:T(8,128)(2,1)}, u32[]{:S(2)}) %copy-start.1) | copy-done | bytes 2097176
  5.4 0.0 copy-start.2
  5.4 0.9 copy-done.2
  6.3 0.0 copy-start.3
  6.3 0.8 copy-done.3
  7.1 0.0 copy-start.4
  7.1 0.7 copy-done.4
  7.8 0.0 copy-start.5
  7.8 0.7 copy-done.5
  8.5 101.2 %distill.1 = (f32[1,256]{1,0:T(1,128)S(1)}, bf16[8,5120]{1,0:T(8,128)(2,1)S(1)}) custom-call(bf16[8,4096]{1,0:T(8,128)(2,1)S(1)} %copy-done.3, bf16[8,5120]{1,0:T(8,128)(2,1)S(1)} %copy-done.2, bf16[1,4096]{1,0:T(2,128)(2,1)S(1)} %reshape.16.teacher_gain, bf16[1,5120]{1,0:T(2,128)(2,1)S(1)} %reshape.17.student_gain, bf16[4096,256]{1,0:T(8,128)(2,1)S(1)} %copy-done.1, ...), custom_call_target="tpu_custom_call" | custom-call | tf_op jit(solution)/shard_map/distill/pallas_call | solution.py:548
  109.7 0.6 copy.12
  110.3 0.6 copy.13
Async XLA Ops:
  2.1 1.7 %copy-start = (bf16[5120,256]{1,0:T(8,128)(2,1)S(1)}, bf16[5120,256]{1,0:T(8,128)(2,1)}, u32[]{:S(2)}) copy-start(bf16[5120,256]{1,0:T(8,128)(2,1)} %student_head.1) | copy-start | bytes 7864324
  3.8 1.6 %copy-start.1 = (bf16[4096,256]{1,0:T(8,128)(2,1)S(1)}, bf16[4096,256]{1,0:T(8,128)(2,1)}, u32[]{:S(2)}) copy-start(bf16[4096,256]{1,0:T(8,128)(2,1)} %teacher_head.1) | copy-start | bytes 6291460
  5.4 0.9 copy-start.2
  6.3 0.8 copy-start.3
  7.1 0.7 copy-start.4
  7.8 0.7 copy-start.5

commit v2 on v0

v2 whole, which is shorter than its diff:
```python
import functools

import jax
import jax.numpy as jnp
from jax import lax
from jax.experimental import pallas as pl
from jax.experimental.pallas import tpu as pltpu
from jax.sharding import PartitionSpec as P

MESH = pl.DeviceIdType.MESH
epsilon = 1e-06
loss_scale = 16.0
distill_mix = 0.5

RING = 4
CORES = 2
BLOCKS = RING * RING
SUB = 16
STEPS = (0, -1, 1, 2)
GATHER_COPIES = 6 + 6 * RING


def contract_last(left_side, right_side):
    return lax.dot_general(
        left_side, right_side, (((1,), (1,)), ((), ())), preferred_element_type=jnp.float32
    )


class Place:
    def __init__(self):
        self.group = lax.axis_index("group")
        self.vocab = lax.axis_index("vocab")
        self.core = lax.rem(self.vocab, CORES)
        self.zh = lax.rem(self.vocab // CORES, RING)
        self.x = self.vocab // (CORES * RING)

    def block(self, dx, dz):
        xx, zz = lax.rem(self.x + dx + RING, RING), lax.rem(self.zh + dz + RING, RING)
        return xx * RING + zz

    def dev(self, dx, dz):
        return (self.group, self.block(dx, dz) * CORES + self.core)

    def nth(self, d):
        return (self.group, lax.rem(self.block(0, 0) + d, BLOCKS) * CORES + self.core)

    def other(self):
        return (self.group, self.block(0, 0) * CORES + 1 - self.core)


class Gather:
    def __init__(self, buf, sem, place, sends):
        self.buf, self.sem, self.place, self.sends = buf, sem, place, sends
        self.width = buf.shape[2] // 2

    def copy(self, index, dx, dz, h, dev):
        view = self.buf.at[self.place.block(dx, dz), :, pl.ds(h * self.width, self.width)]
        return pltpu.make_async_remote_copy(
            src_ref=view,
            dst_ref=view,
            send_sem=self.sem.at[0, index],
            recv_sem=self.sem.at[1, index],
            device_id=dev,
            device_id_type=MESH,
        )

    def go(self, *args):
        copy = self.copy(*args)
        copy.start()
        self.sends.append(copy)

    def wait(self, index, dx, dz, h):
        self.copy(index, dx, dz, h, self.place.dev(1, 0)).wait_recv()

    def start(self):
        up, down = self.place.dev(0, 1), self.place.dev(0, -1)
        self.go(0, 0, 0, 0, up)
        self.go(2, 0, 0, 1, down)
        self.go(1, 0, 0, 1, up)
        self.go(3, 0, 0, 0, down)
        self.x_near(0)

    def x_near(self, j):
        up, down = self.place.dev(1, 0), self.place.dev(-1, 0)
        base, dz = 6 + 6 * j, STEPS[j]
        self.go(base, 0, dz, 0, up)
        self.go(base + 2, 0, dz, 1, down)
        self.go(base + 1, 0, dz, 1, up)
        self.go(base + 3, 0, dz, 0, down)

    def z_forward(self):
        self.wait(0, 0, -1, 0)
        self.go(4, 0, -1, 0, self.place.dev(0, 1))
        self.wait(2, 0, 1, 1)
        self.go(5, 0, 1, 1, self.place.dev(0, -1))

    def z_near(self):
        self.wait(1, 0, -1, 1)
        self.x_near(1)
        self.wait(3, 0, 1, 0)
        self.x_near(2)

    def z_far(self, direct):
        up, down, opposite = self.place.dev(1, 0), self.place.dev(-1, 0), self.place.dev(2, 0)
        base = 6 + 6 * 3
        self.wait(4, 0, 2, 0)
        if direct:
            self.go(base + 4, 0, 2, 0, opposite)
        self.go(base, 0, 2, 0, up)
        self.go(base + 3, 0, 2, 0, down)
        self.wait(5, 0, 2, 1)
        if direct:
            self.go(base + 5, 0, 2, 1, opposite)
        self.go(base + 2, 0, 2, 1, down)
        self.go(base + 1, 0, 2, 1, up)

    def x_forward(self, j):
        base, dz = 6 + 6 * j, STEPS[j]
        self.wait(base, -1, dz, 0)
        self.go(base + 4, -1, dz, 0, self.place.dev(1, 0))
        self.wait(base + 2, 1, dz, 1)
        self.go(base + 5, 1, dz, 1, self.place.dev(-1, 0))

    def x_done(self, j, direct=False):
        base, dz = 6 + 6 * j, STEPS[j]
        if direct:
            self.wait(base, -1, dz, 0)
            self.wait(base + 2, 1, dz, 1)
        self.wait(base + 1, -1, dz, 1)
        self.wait(base + 3, 1, dz, 0)
        self.wait(base + 4, 2, dz, 0)
        self.wait(base + 5, 2, dz, 1)


def kernel(
    groups,
    teacher_rows_in,
    student_rows_in,
    teacher_gain_in,
    student_gain_in,
    teacher_head,
    student_head,
    route_in,
    target_in,
    loss_out,
    grad_out,
    teacher_rows,
    student_rows,
    teacher_gain,
    student_gain,
    route,
    target,
    head_t,
    head_s,
    rows_t,
    rows_s,
    wide,
    out_rows,
    in_rows,
    routed,
    hat_keep,
    inverse_keep,
    target_keep,
    logits_t,
    logits_s,
    exp_s,
    stat_all,
    columns_keep,
    part,
    xf_out,
    xf_in,
    xn_out,
    xn_in,
    z_part,
    zf_out,
    zf_in,
    zn_out,
    zn_in,
    local_sem,
    head_sem,
    route_sem,
    gather_t_sem,
    gather_s_sem,
    stat_sem,
    back_sem,
):
    p = Place()
    g, v, core = p.group, p.vocab, p.core
    f32, bf16 = jnp.float32, jnp.bfloat16
    local_rows, dt = teacher_rows.shape
    ds = student_rows.shape[1]
    shard = head_s.shape[2]
    ht, hs = dt // 2, ds // 2
    qs = hs // 2
    rows = BLOCKS * local_rows
    chunk = dt // SUB
    sends = []

    def remote(src, dst, sem, index, dev):
        copy = pltpu.make_async_remote_copy(
            src_ref=src,
            dst_ref=dst,
            send_sem=sem.at[0, index],
            recv_sem=sem.at[1, index],
            device_id=dev,
            device_id_type=MESH,
        )
        copy.start()
        sends.append(copy)
        return copy

    def fetch(src, dst, index):
        copy = pltpu.make_async_copy(src, dst, local_sem.at[index])
        copy.start()
        return copy

    barrier = pltpu.get_barrier_semaphore()

    def greet(dev):
        pl.semaphore_signal(barrier, inc=1, device_id=dev, device_id_type=MESH)

    for d in range(1, BLOCKS):
        greet(p.nth(d))
    greet(p.other())
    for d in range(1, groups):
        greet((lax.rem(g + d, groups), v))

    load_rows_s = fetch(student_rows_in, student_rows, 0)
    load_gain_s = fetch(student_gain_in, student_gain, 1)
    load_rows_t = fetch(teacher_rows_in, teacher_rows, 2)
    load_gain_t = fetch(teacher_gain_in, teacher_gain, 3)
    load_route = fetch(route_in, route, 4)
    load_target = fetch(target_in, target, 5)
    load_head_s = fetch(student_head, head_s.at[core], 6)
    load_head_t = fetch(teacher_head, head_t.at[core], 7)

    load_rows_s.wait()
    load_gain_s.wait()
    here = p.block(0, 0)
    wide_s = student_rows[...].astype(f32)
    inverse = lax.rsqrt(jnp.mean(wide_s * wide_s, axis=1, keepdims=True) + epsilon)
    inverse_keep[...] = jnp.broadcast_to(inverse, inverse_keep.shape)
    hat = wide_s * inverse
    hat_keep[...] = hat
    gain_s = student_gain[...].astype(f32).reshape(1, ds)
    normed_s = hat * gain_s
    rows_s[here] = jnp.concatenate([normed_s[:, :hs], normed_s[:, hs:]], axis=0).astype(bf16)

    pl.semaphore_wait(barrier, groups - 1 + BLOCKS - 1 + 1)

    student = Gather(rows_s, gather_s_sem, p, sends)
    teacher = Gather(rows_t, gather_t_sem, p, sends)
    student.start()

    load_rows_t.wait()
    load_gain_t.wait()
    load_route.wait()
    wide_t = teacher_rows[...].astype(f32)
    inverse_t = lax.rsqrt(jnp.mean(wide_t * wide_t, axis=1, keepdims=True) + epsilon)
    normed_t = wide_t * inverse_t * teacher_gain[...].astype(f32).reshape(1, dt)
    for c in range(SUB):
        wide[:, c, :] = normed_t[:, c * chunk : (c + 1) * chunk]
    span = lax.axis_size("vocab") * local_rows
    first = g * span + v * local_rows
    my_routes = [route[first + k] for k in range(local_rows)]

    @pl.loop(0, groups)
    def _(dest):
        total = jnp.zeros((SUB, chunk), f32)
        for k in range(local_rows):
            total += jnp.where(my_routes[k] == dest, 1.0, 0.0) * wide[k]
        out_rows[dest] = total.astype(bf16)

    in_rows[g] = out_rows[g]
    routed_copies = []
    for d in range(1, groups):
        dest = lax.rem(g + d, groups)
        routed_copies.append(
            remote(out_rows.at[dest], in_rows.at[g], route_sem, d, (dest, v))
        )
    fetch_head_s = remote(student_head, head_s.at[core], head_sem, 0, p.other())
    fetch_head_t = remote(teacher_head, head_t.at[core], head_sem, 1, p.other())

    student.z_forward()

    ranks, valids = [], []
    seen = jnp.int32(0)
    for t in range(groups):
        start = t * span + v * local_rows
        valid = jnp.int32(0)
        for k in range(local_rows):
            valid += jnp.where(route[start + k] == g, 1, 0)
        ranks.append(seen)
        valids.append(valid)
        seen = seen + valid
    for copy in routed_copies:
        copy.wait_recv()
    for j in range(local_rows):
        total = jnp.zeros((SUB, chunk), f32)
        for t in range(groups):
            weight = jnp.where(ranks[t] == j, valids[t], 0).astype(f32)
            total += weight * in_rows[t].astype(f32)
        wide[j] = total
    for c in range(SUB):
        half, at = divmod(c * chunk, ht)
        routed[half * 8 : half * 8 + 8, at : at + chunk] = wide[:, c, :]
    rows_t[here] = routed[...].astype(bf16)
    teacher.start()

    student.x_forward(0)
    student.z_near()
    teacher.x_forward(0)
    student.z_far(False)
    student.x_forward(1)
    student.x_forward(2)
    teacher.z_forward()
    student.x_forward(3)
    teacher.z_near()

    load_target.wait()
    all_targets = jnp.transpose(jnp.broadcast_to(target[...].astype(f32), (128, 2 * rows)))
    target_keep[...] = all_targets
    columns = (v // CORES) * (CORES * shard) + lax.broadcasted_iota(
        jnp.int32, (rows, CORES * shard), 1
    )
    my_targets = jnp.concatenate(
        [
            target_keep[pl.ds(pl.multiple_of(b * 16 + core * 8, 8), 8), :]
            for b in range(BLOCKS)
        ],
        axis=0,
    )[:, 0:1].astype(jnp.int32)

    def logits(left, count, head, half):
        parts = []
        for c in range(CORES):
            low = jnp.dot(left, head[c, 0:half, :], preferred_element_type=f32)
            high = jnp.dot(left, head[c, half : 2 * half, :], preferred_element_type=f32)
            low = low.reshape(count, 16, shard)[:, 0:8]
            high = high.reshape(count, 16, shard)[:, 8:16]
            parts.append((low + high).reshape(count * 8, shard))
        return jnp.concatenate(parts, axis=1)

    for j in range(RING):
        student.x_done(j)
    load_head_s.wait()
    fetch_head_s.wait_recv()
    values = logits(rows_s[...].reshape(BLOCKS * 16, hs), BLOCKS, head_s, hs)
    logits_s[...] = values
    top_s = jnp.max(values, axis=1, keepdims=True)
    powers = jnp.exp(values - top_s)
    exp_s[...] = powers
    sum_s = jnp.sum(powers, axis=1, keepdims=True)
    picked = jnp.sum(jnp.where(columns == my_targets, values, 0.0), axis=1, keepdims=True)

    teacher.x_forward(1)
    teacher.x_forward(2)
    teacher.z_far(True)

    def teacher_logits(steps):
        blocks = [p.block(dx, STEPS[j]) for j in steps for dx in range(RING)]
        left = jnp.concatenate([rows_t[b] for b in blocks], axis=0)
        values = logits(left, len(blocks), head_t, ht)
        for i, b in enumerate(blocks):
            logits_t[pl.ds(pl.multiple_of(b * 8, 8), 8), :] = values[i * 8 : i * 8 + 8]

    load_head_t.wait()
    fetch_head_t.wait_recv()
    for j in range(3):
        teacher.x_done(j)
    teacher_logits((0, 1, 2))
    teacher.x_done(3, True)
    teacher_logits((3,))

    values = logits_t[...]
    top_t = jnp.max(values, axis=1, keepdims=True)
    exp_t = jnp.exp(values - top_t)
    sum_t = jnp.sum(exp_t, axis=1, keepdims=True)
    cross = jnp.sum(exp_t * (values - logits_s[...]), axis=1, keepdims=True)

    lane = lax.broadcasted_iota(jnp.int32, (rows, 128), 1)
    packed = jnp.zeros((rows, 128), f32)
    for i, value in enumerate((top_t, top_s, top_t, None, sum_t, sum_s, cross, picked)):
        if value is not None:
            packed = jnp.where(lane == i, value, packed)
    stats = jnp.transpose(packed)[0:8, :]

    stat_all[here] = stats
    copies = [
        remote(stat_all.at[here], stat_all.at[here], stat_sem, d, p.nth(d))
        for d in range(1, BLOCKS)
    ]
    for copy in copies:
        copy.wait_recv()
    parts = [stat_all[i] for i in range(BLOCKS)]
    tops = functools.reduce(jnp.maximum, [part[0:4] for part in parts])
    sums = sum(jnp.exp(part[0:4] - tops) * part[4:8] for part in parts)
    merged = jnp.concatenate([tops, sums], axis=0)
    all_top_t, all_top_s = merged[0:1], merged[1:2]
    all_sum_t, all_sum_s = merged[4:5], merged[5:6]
    scale_t = (loss_scale * distill_mix) * jnp.exp(stats[0:1] - all_top_t) / all_sum_t
    scale_s = loss_scale * jnp.exp(stats[1:2] - all_top_s) / all_sum_s
    lse_t = all_top_t + jnp.log(all_sum_t)
    lse_s = all_top_s + jnp.log(all_sum_s)
    loss = distill_mix * (merged[6:7] / all_sum_t - lse_t + lse_s) + (1.0 - distill_mix) * (
        lse_s - merged[7:8]
    )
    turned = jnp.transpose(
        jnp.concatenate([scale_t, scale_s, loss, jnp.zeros((125, rows), f32)], axis=0)
    )
    columns_keep[core] = turned
    loss_copy = remote(columns_keep.at[core], columns_keep.at[core], head_sem, 2, p.other())
    logit_grad = (
        exp_s[...] * turned[:, 1:2]
        - exp_t * turned[:, 0:1]
        - jnp.where(columns == my_targets, loss_scale * (1.0 - distill_mix), 0.0)
    ).astype(bf16)

    step = qs // 2
    for n in range(ds // step):
        half, at = divmod(n * step, hs)
        block = contract_last(
            logit_grad[:, 0:shard], head_s[0, n * step : (n + 1) * step, :]
        ) + contract_last(logit_grad[:, shard:], head_s[1, n * step : (n + 1) * step, :])
        part[:, half * 8 : half * 8 + 8, at : at + step] = block.reshape(
            BLOCKS, local_rows, step
        )

    order = (2, 1, -1, 0)
    plus_x, minus_x = p.dev(1, 0), p.dev(-1, 0)
    plus_z, minus_z = p.dev(0, 1), p.dev(0, -1)
    cols = (slice(0, qs), slice(qs, hs))
    far_copies, near_copies = {}, {}

    def x_first(i):
        far, up, down = (part.at[p.block(d, order[i])] for d in (2, 1, -1))
        xf_out[i, 0] = far[:, cols[0]].astype(bf16)
        xf_out[i, 1] = far[:, cols[1]].astype(bf16)
        far_copies[i] = (
            remote(xf_out.at[i, 0], xf_in.at[i, 0], back_sem, 2 * i, plus_x),
            remote(xf_out.at[i, 1], xf_in.at[i, 1], back_sem, 1 + 2 * i, minus_x),
        )
        xn_out[i, 0, 1] = up[:, cols[1]].astype(bf16)
        xn_out[i, 1, 0] = down[:, cols[0]].astype(bf16)
        near_copies[i] = [
            remote(xn_out.at[i, 0, 1], xn_in.at[i, 0, 1], back_sem, 8 + 2 * i, plus_x),
            remote(xn_out.at[i, 1, 0], xn_in.at[i, 1, 0], back_sem, 9 + 2 * i, minus_x),
        ]

    def x_second(i):
        up, down = (part.at[p.block(d, order[i])] for d in (1, -1))
        far_copies[i][0].wait_recv()
        xn_out[i, 0, 0] = (up[:, cols[0]] + xf_in[i, 0].astype(f32)).astype(bf16)
        near_copies[i].append(
            remote(xn_out.at[i, 0, 0], xn_in.at[i, 0, 0], back_sem, 16 + 2 * i, plus_x)
        )
        far_copies[i][1].wait_recv()
        xn_out[i, 1, 1] = (down[:, cols[1]] + xf_in[i, 1].astype(f32)).astype(bf16)
        near_copies[i].append(
            remote(xn_out.at[i, 1, 1], xn_in.at[i, 1, 1], back_sem, 17 + 2 * i, minus_x)
        )

    def x_done(i):
        for copy in near_copies[i]:
            copy.wait_recv()
        block = part.at[p.block(0, order[i])]
        return [
            block[:, cols[h]] + xn_in[i, 0, h].astype(f32) + xn_in[i, 1, h].astype(f32)
            for h in range(2)
        ]

    x_first(0)
    x_first(1)
    x_second(0)
    x_first(2)
    x_second(1)
    x_first(3)
    x_second(2)
    z_far = []
    for h, value in enumerate(x_done(0)):
        zf_out[h] = value.astype(bf16)
        z_far.append(
            remote(zf_out.at[h], zf_in.at[h], back_sem, 24 + h, (plus_z, minus_z)[h])
        )
    x_second(3)
    up = x_done(1)
    zn_out[0, 1] = up[1].astype(bf16)
    z_near = [remote(zn_out.at[0, 1], zn_in.at[0, 1], back_sem, 26, plus_z)]
    z_part[0] = up[0]
    down = x_done(2)
    zn_out[1, 0] = down[0].astype(bf16)
    z_near.append(remote(zn_out.at[1, 0], zn_in.at[1, 0], back_sem, 27, minus_z))
    z_part[1] = down[1]
    z_far[0].wait_recv()
    zn_out[0, 0] = (z_part[0] + zf_in[0].astype(f32)).astype(bf16)
    z_near.append(remote(zn_out.at[0, 0], zn_in.at[0, 0], back_sem, 28, plus_z))
    z_far[1].wait_recv()
    zn_out[1, 1] = (z_part[1] + zf_in[1].astype(f32)).astype(bf16)
    z_near.append(remote(zn_out.at[1, 1], zn_in.at[1, 1], back_sem, 29, minus_z))
    for h, value in enumerate(x_done(3)):
        z_part[2 + h] = value

    loss_copy.wait_recv()
    both = jnp.concatenate(
        [columns_keep[c, b * 8 : b * 8 + 8, :] for b in range(BLOCKS) for c in range(CORES)],
        axis=0,
    )
    loss_out[...] = jnp.transpose(both)[2:3, :]
    inverse = inverse_keep[:, 0:1]
    hat = hat_keep[...]
    gain = student_gain[...].astype(f32).reshape(1, ds)

    for copy in z_near:
        copy.wait_recv()
    mine = [
        z_part[2 + h] + zn_in[0, h].astype(f32) + zn_in[1, h].astype(f32) for h in range(2)
    ]
    scaled = (
        jnp.concatenate([mine[0][0:8], mine[1][0:8], mine[0][8:16], mine[1][8:16]], axis=1)
        * gain
    )
    grad_out[...] = (
        inverse * (scaled - hat * jnp.mean(scaled * hat, axis=1, keepdims=True))
    ).astype(bf16)

    for copy in sends:
        copy.wait_send()


def local(
    teacher_rows,
    student_rows,
    teacher_gain,
    student_gain,
    teacher_head,
    student_head,
    route,
    target,
):
    groups = lax.axis_size("group")
    f32, bf16 = jnp.float32, jnp.bfloat16
    local_rows, dt = teacher_rows.shape
    ds = student_rows.shape[1]
    shard = teacher_head.shape[1]
    all_rows = target.shape[0]
    rows = all_rows // CORES
    ht, hs = dt // 2, ds // 2
    qs, chunk = hs // 2, dt // SUB
    vmem = pl.BlockSpec(memory_space=pltpu.VMEM)
    anywhere = pl.BlockSpec(memory_space=pl.ANY)
    loss, grad = pl.pallas_call(
        functools.partial(kernel, groups),
        out_shape=(
            jax.ShapeDtypeStruct((1, all_rows), f32),
            jax.ShapeDtypeStruct((local_rows, ds), bf16),
        ),
        in_specs=[anywhere] * 8,
        out_specs=(vmem, vmem),
        scratch_shapes=[
            pltpu.VMEM((local_rows, dt), bf16),
            pltpu.VMEM((local_rows, ds), bf16),
            pltpu.VMEM((dt,), bf16),
            pltpu.VMEM((ds,), bf16),
            pltpu.SMEM(route.shape, jnp.int32),
            pltpu.VMEM((1, all_rows), jnp.int32),
            pltpu.VMEM((CORES, dt, shard), bf16),
            pltpu.VMEM((CORES, ds, shard), bf16),
            pltpu.VMEM((BLOCKS, 16, ht), bf16),
            pltpu.VMEM((BLOCKS, 16, hs), bf16),
            pltpu.VMEM((local_rows, SUB, chunk), f32),
            pltpu.VMEM((groups, SUB, chunk), bf16),
            pltpu.VMEM((groups, SUB, chunk), bf16),
            pltpu.VMEM((16, ht), f32),
            pltpu.VMEM((local_rows, ds), f32),
            pltpu.VMEM((local_rows, 128), f32),
            pltpu.VMEM((all_rows, 128), f32),
            pltpu.VMEM((rows, CORES * shard), f32),
            pltpu.VMEM((rows, CORES * shard), f32),
            pltpu.VMEM((rows, CORES * shard), f32),
            pltpu.VMEM((BLOCKS, 8, rows), f32),
            pltpu.VMEM((CORES, rows, 128), f32),
            pltpu.VMEM((BLOCKS, 16, hs), f32),
            pltpu.VMEM((4, 2, 16, qs), bf16),
            pltpu.VMEM((4, 2, 16, qs), bf16),
            pltpu.VMEM((4, 2, 2, 16, qs), bf16),
            pltpu.VMEM((4, 2, 2, 16, qs), bf16),
            pltpu.VMEM((4, 16, qs), f32),
            pltpu.VMEM((2, 16, qs), bf16),
            pltpu.VMEM((2, 16, qs), bf16),
            pltpu.VMEM((2, 2, 16, qs), bf16),
            pltpu.VMEM((2, 2, 16, qs), bf16),
            pltpu.SemaphoreType.DMA((8,)),
            pltpu.SemaphoreType.DMA((2, 3)),
            pltpu.SemaphoreType.DMA((2, groups)),
            pltpu.SemaphoreType.DMA((2, GATHER_COPIES)),
            pltpu.SemaphoreType.DMA((2, GATHER_COPIES)),
            pltpu.SemaphoreType.DMA((2, BLOCKS)),
            pltpu.SemaphoreType.DMA((2, 30)),
        ],
        compiler_params=pltpu.CompilerParams(
            collective_id=0, has_side_effects=True, vmem_limit_bytes=60 * 1024 * 1024
        ),
        name="distill",
    )(
        teacher_rows,
        student_rows,
        teacher_gain,
        student_gain,
        teacher_head,
        student_head,
        route,
        target.reshape(1, all_rows),
    )
    return (loss.reshape(all_rows), grad)


def solution(mesh):
    placed = (
        P(("group", "vocab"), None),
        P(("group", "vocab"), None),
        P(),
        P(),
        P(None, "vocab"),
        P(None, "vocab"),
        P(),
        P("group"),
    )
    return jax.shard_map(
        local,
        mesh=mesh,
        in_specs=placed,
        out_specs=(P("group"), P(("group", "vocab"), None)),
        check_vma=False,
    )
```

time: 496 us -> 89.5 us (0.18)
  waiting for transfers between devices: 278 us -> 0 us
  blocking collectives: 171 us -> 0 us
  Pallas kernels: 0 us -> 85 us
  between operations: 13.8 us -> 0.64 us
  matrix products: 10.5 us -> 0 us
  other arithmetic: 9.97 us -> 0 us
  starting transfers between devices: 9.03 us -> 0 us
    all_gather x2 -> x0, waiting for transfers between devices: 155 us -> none  [the longest x1 78.4 us: local(): lax.all_gather(student_normed, 'vocab', axis=0, tiled=True)]
    reduce_scatter x1 -> x0, waiting for transfers between devices: 117 us -> none  [local(): lax.psum_scatter(contract_last(logit_grad, student_head).astype(jnp.bfloa...]
    pmax x1 -> x0, blocking collectives: 87.1 us -> none  [local(): lax.pmax((jnp.max(teacher_logits, axis=1), jnp.max(student_logits, axis=1...]
    pallas_call x0 -> x1, Pallas kernels: none -> 85 us  [local(): pl.pallas_call(functools.partial(kernel, groups), out_shape=(jax.ShapeDty...]
    psum x1 -> x0, blocking collectives: 84.2 us -> none  [local(): lax.psum((jnp.sum(teacher_exp, axis=1), jnp.sum(student_exp, axis=1), jnp...]
    dot_general x5 -> x0, matrix products: 10.5 us -> none  [the longest x1 3.16 us: local(): jnp.dot(lax.all_gather(routed, 'vocab', axis=0, tiled=True), teacher_head...]
    all_to_all x1 -> x0, starting transfers between devices: 8.91 us -> none  [local(): lax.all_to_all(outgoing, 'group', split_axis=0, concat_axis=0, tiled=True)]
    all_to_all x1 -> x0, waiting for transfers between devices: 5.58 us -> none  [local(): lax.all_to_all(outgoing, 'group', split_axis=0, concat_axis=0, tiled=True)]
  transfers between devices with their start and end apart: 4 -> 0, of which waited for: 4 -> 0; matrix products, arithmetic and copies ran while one was open for 2% -> 0% of each run, Pallas kernels for 0% -> 0%
where the time goes in v2:
time: 89.5 us; the launch traced here: 88.4 us
  Pallas kernels  85 us (95%)
  local copies, waits for them, and re-layouts  2.75 us (3%)
    pallas_call x1, Pallas kernels, local(): pl.pallas_call(functools.partial(kernel, groups), out_shape=(jax.ShapeDty...  85 us
    unnamed x2, local copies, waits for them, and re-layouts  2.75 us

profile of v2, /device:TPU:24, one launch (start us, length us, event | category | flops | bytes accessed | tf_op | source)
XLA Modules:
  0.0 88.4 jit_solution(2629918131623838802)
XLA Ops:
  0.6 85.0 %distill.1 = (f32[1,256]{1,0:T(1,128)}, bf16[8,5120]{1,0:T(8,128)(2,1)}) custom-call(bf16[8,4096]{1,0:T(8,128)(2,1)} %teacher_rows_in.1, bf16[8,5120]{1,0:T(8,128)(2,1)} %student_rows_in.1, bf16[4096]{0:T(1024)(128)(2,1)} %teacher_gain_in.1, bf16[5120]{0:T(1024)(128)(2,1)} %student_gain_in.1, bf16[4096,256]{1,0:T(8,128)(2,1)} %teacher_head.1, ...), custom_call_target="tpu_custom_call" | custom-call | tf_op jit(solution)/shard_map/distill/pallas_call | solution.py:551
  85.6 1.2 %copy.12 = f32[256]{0:T(256)} copy(f32[256]{0:T(256)} %bitcast.3) | data formatting | bytes 2048
  86.8 1.5 %copy.13 = bf16[8,5120]{1,0:T(8,128)(2,1)} copy(bf16[8,5120]{1,0:T(8,128)(2,1)} %get-tuple-element.9) | data formatting | bytes 163840

commit v3 on v2

--- a/solution.py
+++ b/solution.py
@@ -78,27 +78,32 @@
         self.go(2, 0, 0, 1, down)
         self.go(1, 0, 0, 1, up)
         self.go(3, 0, 0, 0, down)
-        self.x_near(0)
-
-    def x_near(self, j):
+        self.x_half(0, 0)
+        self.x_half(0, 1)
+
+    def x_half(self, j, h):
         up, down = self.place.dev(1, 0), self.place.dev(-1, 0)
         base, dz = 6 + 6 * j, STEPS[j]
-        self.go(base, 0, dz, 0, up)
-        self.go(base + 2, 0, dz, 1, down)
-        self.go(base + 1, 0, dz, 1, up)
-        self.go(base + 3, 0, dz, 0, down)
+        if h == 0:
+            self.go(base, 0, dz, 0, up)
+            self.go(base + 3, 0, dz, 0, down)
+        else:
+            self.go(base + 2, 0, dz, 1, down)
+            self.go(base + 1, 0, dz, 1, up)
 
     def z_forward(self):
         self.wait(0, 0, -1, 0)
         self.go(4, 0, -1, 0, self.place.dev(0, 1))
+        self.x_half(1, 0)
         self.wait(2, 0, 1, 1)
         self.go(5, 0, 1, 1, self.place.dev(0, -1))
+        self.x_half(2, 1)
 
     def z_near(self):
         self.wait(1, 0, -1, 1)
-        self.x_near(1)
+        self.x_half(1, 1)
         self.wait(3, 0, 1, 0)
-        self.x_near(2)
+        self.x_half(2, 0)
 
     def z_far(self, direct):
         up, down, opposite = self.place.dev(1, 0), self.place.dev(-1, 0), self.place.dev(2, 0)
@@ -219,12 +224,6 @@
     def greet(dev):
         pl.semaphore_signal(barrier, inc=1, device_id=dev, device_id_type=MESH)
 
-    for d in range(1, BLOCKS):
-        greet(p.nth(d))
-    greet(p.other())
-    for d in range(1, groups):
-        greet((lax.rem(g + d, groups), v))
-
     load_rows_s = fetch(student_rows_in, student_rows, 0)
     load_gain_s = fetch(student_gain_in, student_gain, 1)
     load_rows_t = fetch(teacher_rows_in, teacher_rows, 2)
@@ -233,6 +232,13 @@
     load_target = fetch(target_in, target, 5)
     load_head_s = fetch(student_head, head_s.at[core], 6)
     load_head_t = fetch(teacher_head, head_t.at[core], 7)
+    for d in range(1, RING):
+        greet(p.dev(d, 0))
+    greet(p.dev(0, 1))
+    greet(p.dev(0, -1))
+    greet(p.other())
+    for d in range(1, groups):
+        greet((lax.rem(g + d, groups), v))
 
     load_rows_s.wait()
     load_gain_s.wait()
@@ -246,7 +252,7 @@
     normed_s = hat * gain_s
     rows_s[here] = jnp.concatenate([normed_s[:, :hs], normed_s[:, hs:]], axis=0).astype(bf16)
 
-    pl.semaphore_wait(barrier, groups - 1 + BLOCKS - 1 + 1)
+    pl.semaphore_wait(barrier, groups - 1 + RING - 1 + 2 + 1)
 
     student = Gather(rows_s, gather_s_sem, p, sends)
     teacher = Gather(rows_t, gather_t_sem, p, sends)
@@ -341,6 +347,9 @@
             parts.append((low + high).reshape(count * 8, shard))
         return jnp.concatenate(parts, axis=1)
 
+    teacher.x_forward(1)
+    teacher.x_forward(2)
+    teacher.z_far(True)
     for j in range(RING):
         student.x_done(j)
     load_head_s.wait()
@@ -353,9 +362,6 @@
     sum_s = jnp.sum(powers, axis=1, keepdims=True)
     picked = jnp.sum(jnp.where(columns == my_targets, values, 0.0), axis=1, keepdims=True)
 
-    teacher.x_forward(1)
-    teacher.x_forward(2)
-    teacher.z_far(True)
 
     def teacher_logits(steps):
         blocks = [p.block(dx, STEPS[j]) for j in steps for dx in range(RING)]
@@ -447,6 +453,18 @@
             remote(xn_out.at[i, 1, 0], xn_in.at[i, 1, 0], back_sem, 9 + 2 * i, minus_x),
         ]
 
+    def x_whole(i):
+        slots = (xf_out.at[i], xn_out.at[i, 0], xn_out.at[i, 1])
+        for slot, d in zip(slots, (2, 1, -1)):
+            block = part.at[p.block(d, order[i])]
+            for h in range(2):
+                slot[h] = block[:, cols[h]].astype(bf16)
+        near_copies[i] = [
+            remote(slots[0], xf_in.at[i], back_sem, 2 * i, p.dev(2, 0)),
+            remote(slots[1], xn_in.at[i, 0], back_sem, 8 + 2 * i, plus_x),
+            remote(slots[2], xn_in.at[i, 1], back_sem, 9 + 2 * i, minus_x),
+        ]
+
     def x_second(i):
         up, down = (part.at[p.block(d, order[i])] for d in (1, -1))
         far_copies[i][0].wait_recv()
@@ -469,16 +487,15 @@
             for h in range(2)
         ]
 
-    x_first(0)
+    x_whole(0)
     x_first(1)
-    x_second(0)
     x_first(2)
+    x_first(3)
     x_second(1)
-    x_first(3)
     x_second(2)
     z_far = []
     for h, value in enumerate(x_done(0)):
-        zf_out[h] = value.astype(bf16)
+        zf_out[h] = (value + xf_in[0, h].astype(f32)).astype(bf16)
         z_far.append(
             remote(zf_out.at[h], zf_in.at[h], back_sem, 24 + h, (plus_z, minus_z)[h])
         )

time: 89.5 us -> 85.1 us (0.951)
  the two profiles are of different devices: /device:TPU:24 before, /device:TPU:32 now
where the time goes in v3:
time: 85.1 us; the launch traced here: 84.9 us
  Pallas kernels  81.5 us (96%)
  local copies, waits for them, and re-layouts  2.75 us (3%)
    pallas_call x1, Pallas kernels, local(): pl.pallas_call(functools.partial(kernel, groups), out_shape=(jax.ShapeDty...  81.5 us
    unnamed x2, local copies, waits for them, and re-layouts  2.75 us

profile of v3, /device:TPU:32, one launch (start us, length us, event | category | flops | bytes accessed | tf_op | source)
XLA Modules:
  0.0 84.9 jit_solution(12669134659998295442)
XLA Ops:
  0.6 81.5 %distill.1 = (f32[1,256]{1,0:T(1,128)}, bf16[8,5120]{1,0:T(8,128)(2,1)}) custom-call(bf16[8,4096]{1,0:T(8,128)(2,1)} %teacher_rows_in.1, bf16[8,5120]{1,0:T(8,128)(2,1)} %student_rows_in.1, bf16[4096]{0:T(1024)(128)(2,1)} %teacher_gain_in.1, bf16[5120]{0:T(1024)(128)(2,1)} %student_gain_in.1, bf16[4096,256]{1,0:T(8,128)(2,1)} %teacher_head.1, ...), custom_call_target="tpu_custom_call" | custom-call | tf_op jit(solution)/shard_map/distill/pallas_call | solution.py:568
  82.1 1.2 %copy.12 = f32[256]{0:T(256)} copy(f32[256]{0:T(256)} %bitcast.3) | data formatting | bytes 2048
  83.4 1.5 %copy.13 = bf16[8,5120]{1,0:T(8,128)(2,1)} copy(bf16[8,5120]{1,0:T(8,128)(2,1)} %get-tuple-element.9) | data formatting | bytes 163840

commit v4 on v3

--- a/solution.py
+++ b/solution.py
@@ -252,12 +252,6 @@
     normed_s = hat * gain_s
     rows_s[here] = jnp.concatenate([normed_s[:, :hs], normed_s[:, hs:]], axis=0).astype(bf16)
 
-    pl.semaphore_wait(barrier, groups - 1 + RING - 1 + 2 + 1)
-
-    student = Gather(rows_s, gather_s_sem, p, sends)
-    teacher = Gather(rows_t, gather_t_sem, p, sends)
-    student.start()
-
     load_rows_t.wait()
     load_gain_t.wait()
     load_route.wait()
@@ -278,6 +272,12 @@
         out_rows[dest] = total.astype(bf16)
 
     in_rows[g] = out_rows[g]
+    pl.semaphore_wait(barrier, groups - 1 + RING - 1 + 2 + 1)
+
+    student = Gather(rows_s, gather_s_sem, p, sends)
+    teacher = Gather(rows_t, gather_t_sem, p, sends)
+    student.start()
+
     routed_copies = []
     for d in range(1, groups):
         dest = lax.rem(g + d, groups)
@@ -287,7 +287,9 @@
     fetch_head_s = remote(student_head, head_s.at[core], head_sem, 0, p.other())
     fetch_head_t = remote(teacher_head, head_t.at[core], head_sem, 1, p.other())
 
+    student.x_forward(0)
     student.z_forward()
+    student.z_near()
 
     ranks, valids = [], []
     seen = jnp.int32(0)
@@ -313,15 +315,13 @@
     rows_t[here] = routed[...].astype(bf16)
     teacher.start()
 
-    student.x_forward(0)
-    student.z_near()
     teacher.x_forward(0)
     student.z_far(False)
     student.x_forward(1)
     student.x_forward(2)
     teacher.z_forward()
+    teacher.z_near()
     student.x_forward(3)
-    teacher.z_near()
 
     load_target.wait()
     all_targets = jnp.transpose(jnp.broadcast_to(target[...].astype(f32), (128, 2 * rows)))

time: 85.1 us -> 83.5 us (0.981)
  the two profiles are of different devices: /device:TPU:32 before, /device:TPU:24 now
where the time goes in v4:
time: 83.5 us; the launch traced here: 81.8 us
  Pallas kernels  78.4 us (94%)
  local copies, waits for them, and re-layouts  2.75 us (3%)
    pallas_call x1, Pallas kernels, local(): pl.pallas_call(functools.partial(kernel, groups), out_shape=(jax.ShapeDty...  78.4 us
    unnamed x2, local copies, waits for them, and re-layouts  2.75 us

profile of v4, /device:TPU:24, one launch (start us, length us, event | category | flops | bytes accessed | tf_op | source)
XLA Modules:
  0.0 81.8 jit_solution(3742749227748159694)
XLA Ops:
  0.6 78.4 %distill.1 = (f32[1,256]{1,0:T(1,128)}, bf16[8,5120]{1,0:T(8,128)(2,1)}) custom-call(bf16[8,4096]{1,0:T(8,128)(2,1)} %teacher_rows_in.1, bf16[8,5120]{1,0:T(8,128)(2,1)} %student_rows_in.1, bf16[4096]{0:T(1024)(128)(2,1)} %teacher_gain_in.1, bf16[5120]{0:T(1024)(128)(2,1)} %student_gain_in.1, bf16[4096,256]{1,0:T(8,128)(2,1)} %teacher_head.1, ...), custom_call_target="tpu_custom_call" | custom-call | tf_op jit(solution)/shard_map/distill/pallas_call | solution.py:568
  79.0 1.2 %copy.12 = f32[256]{0:T(256)} copy(f32[256]{0:T(256)} %bitcast.3) | data formatting | bytes 2048
  80.3 1.5 %copy.13 = bf16[8,5120]{1,0:T(8,128)(2,1)} copy(bf16[8,5120]{1,0:T(8,128)(2,1)} %get-tuple-element.9) | data formatting | bytes 163840

commit v5 on v4

--- a/solution.py
+++ b/solution.py
@@ -422,16 +422,6 @@
         - jnp.where(columns == my_targets, loss_scale * (1.0 - distill_mix), 0.0)
     ).astype(bf16)
 
-    step = qs // 2
-    for n in range(ds // step):
-        half, at = divmod(n * step, hs)
-        block = contract_last(
-            logit_grad[:, 0:shard], head_s[0, n * step : (n + 1) * step, :]
-        ) + contract_last(logit_grad[:, shard:], head_s[1, n * step : (n + 1) * step, :])
-        part[:, half * 8 : half * 8 + 8, at : at + step] = block.reshape(
-            BLOCKS, local_rows, step
-        )
-
     order = (2, 1, -1, 0)
     plus_x, minus_x = p.dev(1, 0), p.dev(-1, 0)
     plus_z, minus_z = p.dev(0, 1), p.dev(0, -1)
@@ -453,17 +443,15 @@
             remote(xn_out.at[i, 1, 0], xn_in.at[i, 1, 0], back_sem, 9 + 2 * i, minus_x),
         ]
 
-    def x_whole(i):
-        slots = (xf_out.at[i], xn_out.at[i, 0], xn_out.at[i, 1])
+    def x_whole(i, h):
+        slots = (xf_out.at[i, h], xn_out.at[i, 0, h], xn_out.at[i, 1, h])
         for slot, d in zip(slots, (2, 1, -1)):
-            block = part.at[p.block(d, order[i])]
-            for h in range(2):
-                slot[h] = block[:, cols[h]].astype(bf16)
-        near_copies[i] = [
-            remote(slots[0], xf_in.at[i], back_sem, 2 * i, p.dev(2, 0)),
-            remote(slots[1], xn_in.at[i, 0], back_sem, 8 + 2 * i, plus_x),
-            remote(slots[2], xn_in.at[i, 1], back_sem, 9 + 2 * i, minus_x),
-        ]
+            slot[...] = part[p.block(d, order[i]), :, cols[h]].astype(bf16)
+        return (
+            remote(slots[0], xf_in.at[i, h], back_sem, 2 * i + h, p.dev(2, 0)),
+            remote(slots[1], xn_in.at[i, 0, h], back_sem, 16 - 8 * h + 2 * i, plus_x),
+            remote(slots[2], xn_in.at[i, 1, h], back_sem, 9 + 8 * h + 2 * i, minus_x),
+        )
 
     def x_second(i):
         up, down = (part.at[p.block(d, order[i])] for d in (1, -1))
@@ -487,15 +475,33 @@
             for h in range(2)
         ]
 
-    x_whole(0)
+    step = qs // 2
+    whole_copies = []
+    for h in range(2):
+        for n in (2 * h, 2 * h + 1, 2 * h + 4, 2 * h + 5):
+            half, at = divmod(n * step, hs)
+            block = contract_last(
+                logit_grad[:, 0:shard], head_s[0, n * step : (n + 1) * step, :]
+            ) + contract_last(logit_grad[:, shard:], head_s[1, n * step : (n + 1) * step, :])
+            part[:, half * 8 : half * 8 + 8, at : at + step] = block.reshape(
+                BLOCKS, local_rows, step
+            )
+        whole_copies.append(x_whole(0, h))
     x_first(1)
     x_first(2)
     x_first(3)
     x_second(1)
     x_second(2)
     z_far = []
-    for h, value in enumerate(x_done(0)):
-        zf_out[h] = (value + xf_in[0, h].astype(f32)).astype(bf16)
+    for h in range(2):
+        for copy in whole_copies[h]:
+            copy.wait_recv()
+        zf_out[h] = (
+            part[p.block(0, order[0]), :, cols[h]]
+            + xf_in[0, h].astype(f32)
+            + xn_in[0, 0, h].astype(f32)
+            + xn_in[0, 1, h].astype(f32)
+        ).astype(bf16)
         z_far.append(
             remote(zf_out.at[h], zf_in.at[h], back_sem, 24 + h, (plus_z, minus_z)[h])
         )

time: 83.5 us -> 82.5 us (0.988)
  no operation moved by 1% of the time
where the time goes in v5:
time: 82.5 us; the launch traced here: 81.1 us
  Pallas kernels  77.7 us (94%)
  local copies, waits for them, and re-layouts  2.75 us (3%)
    pallas_call x1, Pallas kernels, local(): pl.pallas_call(functools.partial(kernel, groups), out_shape=(jax.ShapeDty...  77.7 us
    unnamed x2, local copies, waits for them, and re-layouts  2.75 us

profile of v5, /device:TPU:24, one launch (start us, length us, event | category | flops | bytes accessed | tf_op | source)
XLA Modules:
  0.0 81.1 jit_solution(8600435575251383087)
XLA Ops:
  0.6 77.7 %distill.1 = (f32[1,256]{1,0:T(1,128)}, bf16[8,5120]{1,0:T(8,128)(2,1)}) custom-call(bf16[8,4096]{1,0:T(8,128)(2,1)} %teacher_rows_in.1, bf16[8,5120]{1,0:T(8,128)(2,1)} %student_rows_in.1, bf16[4096]{0:T(1024)(128)(2,1)} %teacher_gain_in.1, bf16[5120]{0:T(1024)(128)(2,1)} %student_gain_in.1, bf16[4096,256]{1,0:T(8,128)(2,1)} %teacher_head.1, ...), custom_call_target="tpu_custom_call" | custom-call | tf_op jit(solution)/shard_map/distill/pallas_call | solution.py:574
  78.4 1.2 %copy.12 = f32[256]{0:T(256)} copy(f32[256]{0:T(256)} %bitcast.3) | data formatting | bytes 2048
  79.6 1.5 %copy.13 = bf16[8,5120]{1,0:T(8,128)(2,1)} copy(bf16[8,5120]{1,0:T(8,128)(2,1)} %get-tuple-element.9) | data formatting | bytes 163840

commit v6 on v5

--- a/solution.py
+++ b/solution.py
@@ -125,6 +125,12 @@
         self.go(base + 4, -1, dz, 0, self.place.dev(1, 0))
         self.wait(base + 2, 1, dz, 1)
         self.go(base + 5, 1, dz, 1, self.place.dev(-1, 0))
+
+    def x_last(self, h):
+        base, dz = 6 + 6 * 3, STEPS[3]
+        self.wait(base + h, -1, dz, h)
+        self.wait(base + 3 - h, 1, dz, h)
+        self.wait(base + 4 + h, 2, dz, h)
 
     def x_done(self, j, direct=False):
         base, dz = 6 + 6 * j, STEPS[j]
@@ -375,8 +381,20 @@
     for j in range(3):
         teacher.x_done(j)
     teacher_logits((0, 1, 2))
-    teacher.x_done(3, True)
-    teacher_logits((3,))
+    blocks = [p.block(dx, STEPS[3]) for dx in range(RING)]
+    sums = [0.0] * CORES
+    for h in range(2):
+        teacher.x_last(h)
+        near, far = h * (ht // 2), ht + h * (ht // 2)
+        left = jnp.concatenate([rows_t[b, :, near : near + ht // 2] for b in blocks], axis=0)
+        for c in range(CORES):
+            low = jnp.dot(left, head_t[c, near : near + ht // 2, :], preferred_element_type=f32)
+            high = jnp.dot(left, head_t[c, far : far + ht // 2, :], preferred_element_type=f32)
+            low, high = (value.reshape(RING, 16, shard) for value in (low, high))
+            sums[c] = sums[c] + (low[:, 0:8] + high[:, 8:16]).reshape(RING * 8, shard)
+    values = jnp.concatenate(sums, axis=1)
+    for i, b in enumerate(blocks):
+        logits_t[pl.ds(pl.multiple_of(b * 8, 8), 8), :] = values[i * 8 : i * 8 + 8]
 
     values = logits_t[...]
     top_t = jnp.max(values, axis=1, keepdims=True)

time: 82.5 us -> 82.2 us (level)
  no operation moved by 1% of the time
where the time goes in v6:
time: 82.2 us; the launch traced here: 80.8 us
  Pallas kernels  77.4 us (94%)
  local copies, waits for them, and re-layouts  2.75 us (3%)
    pallas_call x1, Pallas kernels, local(): pl.pallas_call(functools.partial(kernel, groups), out_shape=(jax.ShapeDty...  77.4 us
    unnamed x2, local copies, waits for them, and re-layouts  2.75 us

profile of v6, /device:TPU:24, one launch (start us, length us, event | category | flops | bytes accessed | tf_op | source)
XLA Modules:
  0.0 80.8 jit_solution(5115143606526707942)
XLA Ops:
  0.6 77.4 %distill.1 = (f32[1,256]{1,0:T(1,128)}, bf16[8,5120]{1,0:T(8,128)(2,1)}) custom-call(bf16[8,4096]{1,0:T(8,128)(2,1)} %teacher_rows_in.1, bf16[8,5120]{1,0:T(8,128)(2,1)} %student_rows_in.1, bf16[4096]{0:T(1024)(128)(2,1)} %teacher_gain_in.1, bf16[5120]{0:T(1024)(128)(2,1)} %student_gain_in.1, bf16[4096,256]{1,0:T(8,128)(2,1)} %teacher_head.1, ...), custom_call_target="tpu_custom_call" | custom-call | tf_op jit(solution)/shard_map/distill/pallas_call | solution.py:592
  78.0 1.2 %copy.12 = f32[256]{0:T(256)} copy(f32[256]{0:T(256)} %bitcast.3) | data formatting | bytes 2048
  79.2 1.5 %copy.13 = bf16[8,5120]{1,0:T(8,128)(2,1)} copy(bf16[8,5120]{1,0:T(8,128)(2,1)} %get-tuple-element.9) | data formatting | bytes 163840
